TPU v7x, 128 devices: a whole 4x4x4 slice. The times are simulated.
128 devices in a mesh: space: 16 (over z, y_lo, core), tm: 8 (over y_hi, x).
Axes of the slice: x: 4, y: 4 (y_hi: 2, y_lo: 2; y = y_hi * 2 + y_lo), z: 4, core: 2. Of those that a mesh axis runs over, the one named last changes fastest.
Arguments:
- snapshots: bfloat16 [640, 4, 131072], P('tm', None, 'space'), may hold values from -6 to 6
- weights: float32 [131072], P(('space', 'tm')), may hold values from 0.3 to 18, as said below
Outputs:
- modes: bfloat16 [128, 4, 131072], P(None, None, ('space', 'tm'))
- spectra: float32 [128, 8, 8], replicated
Inputs may be any that keep to these rules, and one draw needn't show every extreme that they name: Positive quadrature weights.
All inputs are finite; a program needn't handle non-finite values.
Results may differ from a plain program's by a relative error of at most 0.0047.
Values may be sent and summed in bfloat16 or wider, within the bound.
No kernel may reach another device: no remote copies, remote signals or barrier semaphores. Data moves between devices by JAX's collectives and lax.ppermute only.
A program may use at most 128 MiB of HBM per device.

v0:
```python
import functools
import math

import jax
import jax.numpy as jnp
import ml_dtypes
import numpy as np
from jax import lax
from jax.experimental import pallas as pl
from jax.experimental.pallas import tpu as pltpu
from jax.sharding import PartitionSpec as P

NFFT = 256
BLOCKS = 4
HOP = 128
FREQS = 128
TIME = 640
ROWS = 2 * BLOCKS
GROUP = 32
GROUPS = FREQS // GROUP
AXES = ("space", "tm")
TILE = 256
WIDE = 512
ACROSS = 4
PACKS = (2, 7, 8)
WHOLE = 7
DEPTH = 5
PACK_VMEM = 54 << 20
GRAM_VMEM = 24 << 20
STEPS = ((1, 1), (0, 3), (1, 0), (0, 2), (1, 2), (0, 1), (1, 3), (0, 0))
F32 = jnp.float32
BF16 = jnp.bfloat16


def tables():
    steps = np.arange(NFFT)
    phase = (np.arange(FREQS)[:, None] * steps[None, :] % NFFT) * (2.0 * math.pi / NFFT)
    window = 0.5 - 0.5 * np.cos(steps * (2.0 * math.pi / NFFT))
    full = np.concatenate([window * np.cos(phase), -window * np.sin(phase)], 0)
    full = (full / np.sqrt(np.sum(window * window))).astype(np.float32)
    high = full.astype(ml_dtypes.bfloat16)
    low = (full - high.astype(np.float32)).astype(ml_dtypes.bfloat16)
    split = np.concatenate([high, low], 0)
    sums = (high.astype(np.float64) + low.astype(np.float64)).sum(1, keepdims=True)
    return full, split, sums.astype(np.float32)


def shifted(index, step):
    half, across = index >> 2, index & 3
    return ((half + step[0]) & 1) * ACROSS + ((across + step[1]) & 3)


def parts_of(k):
    return 2 if WHOLE <= k < len(STEPS) - 1 else 1


def pack_kernel(first, end, x_ref, *refs):
    out_refs, (held_ref, sem_ref) = list(refs[:-2]), refs[-2:]
    me = lax.axis_index("tm")
    width = held_ref.shape[3]
    copies = []
    for k in range(first, end):
        lane = pl.multiple_of(shifted(me, STEPS[k]) * width, width)
        copy = pltpu.make_async_copy(
            x_ref.at[:, :, pl.ds(lane, width)], held_ref.at[k - first], sem_ref.at[k - first]
        )
        copy.start()
        copies.append(copy)
    for k in range(first, end):
        copies[k - first].wait()
        size = width // parts_of(k)
        for start in range(0, width, size):
            out_ref = out_refs.pop(0)
            for at in range(0, size, TILE):
                piece = held_ref[k - first, :, :, start + at : start + at + TILE]
                out_ref[:, :, at : at + TILE] = jnp.transpose(piece, (1, 0, 2))


def pack(x, first, end):
    times, count, points = x.shape
    width = points // len(STEPS)
    sizes = [width // parts_of(k) for k in range(first, end) for _ in range(parts_of(k))]
    out = pl.pallas_call(
        functools.partial(pack_kernel, first, end),
        in_specs=[pl.BlockSpec(memory_space=pl.ANY)],
        out_specs=[pl.BlockSpec(memory_space=pltpu.VMEM)] * len(sizes),
        out_shape=[jax.ShapeDtypeStruct((count, times, size), x.dtype) for size in sizes],
        scratch_shapes=[
            pltpu.VMEM((end - first, times, count, width), x.dtype),
            pltpu.SemaphoreType.DMA((end - first,)),
        ],
        compiler_params=pltpu.CompilerParams(
            vmem_limit_bytes=PACK_VMEM if first < len(STEPS) - 1 else GRAM_VMEM
        ),
    )(x)
    out = list(out)
    return [[out.pop(0) for _ in range(parts_of(k))] for k in range(first, end)]


def gram_kernel(start, *refs):
    members = len(STEPS)
    pieces = refs[:members]
    w_ref, split_ref, sums_ref, before_ref = refs[members : members + 4]
    gram_ref, x_ref, mean_ref, coef_ref, acc_ref = refs[members + 4 :]
    me = lax.axis_index("tm")
    count, _, points = x_ref.shape
    steps = pieces[0].shape[1]
    rows = []
    for step in STEPS:
        source = shifted(me, (-step[0], -step[1]))
        rows.append(pl.multiple_of(source * steps, 16))
    acc_ref[...] = jnp.zeros_like(acc_ref)

    for tile in range(points // WIDE):
        here = pl.ds(tile * WIDE, WIDE)
        for k in range(members):
            for v in range(count):
                skip = start if pieces[k].shape[2] > points else 0
                there = pl.ds(skip + tile * WIDE, WIDE)
                x_ref[v, pl.ds(rows[k], steps), here] = pieces[k][v, :, there]
        split = split_ref[...]
        sums = sums_ref[...]
        for v in range(count):
            x = x_ref[v, :, here]
            mean = jnp.sum(x.astype(F32), axis=0, keepdims=True) * (1.0 / TIME)
            mean_ref[v : v + 1, here] = mean
            shift = sums * mean
            for b in range(BLOCKS):
                both = jnp.dot(split, x[b * HOP : b * HOP + NFFT], preferred_element_type=F32)
                coef = (both[:NFFT] + both[NFFT:] - shift).astype(BF16)
                for r in range(2):
                    for g in range(GROUPS):
                        part = coef[r * FREQS + g * GROUP : r * FREQS + (g + 1) * GROUP]
                        c = r * BLOCKS + b
                        coef_ref[g, c * GROUP : (c + 1) * GROUP, v * WIDE : (v + 1) * WIDE] = part
        weights = jnp.concatenate([w_ref[:, pl.ds(start + tile * WIDE, WIDE)]] * count, axis=1)
        for g in range(GROUPS):
            a = coef_ref[g]
            weighted = (a.astype(F32) * weights).astype(BF16)
            acc_ref[g] += lax.dot_general(
                weighted, a, (((1,), (1,)), ((), ())), preferred_element_type=F32
            )

    size = ROWS * GROUP
    row = lax.broadcasted_iota(jnp.int32, (GROUP, size), 0)
    lane = lax.broadcasted_iota(jnp.int32, (GROUP, size), 1)
    same = lane % GROUP == row
    lane1 = lax.broadcasted_iota(jnp.int32, (1, FREQS), 1)
    for g in range(GROUPS):
        last = jnp.zeros((1, FREQS), F32)
        for c in range(ROWS):
            block = acc_ref[g, c * GROUP : (c + 1) * GROUP, :]
            line = jnp.sum(jnp.where(same, block, 0.0), axis=0, keepdims=True)
            if c < BLOCKS:
                mine = lane1 // GROUP == c
                last = last + jnp.where(mine, line[:, FREQS:], 0.0)
            turned = pltpu.roll(line, (size - c * GROUP) % size, 1) if c else line
            at = g * ROWS + c
            gram_ref[at : at + 1, :] = before_ref[at : at + 1, :] + turned[:, :FREQS]
        at = GROUPS * ROWS + g
        gram_ref[at : at + 1, :] = before_ref[at : at + 1, :] + last
    gram_ref[GROUPS * ROWS + GROUPS :, :] = jnp.zeros((ROWS - GROUPS, FREQS), F32)


def gram_terms(pieces, weights, split, sums, before, start, points):
    count = pieces[0].shape[0]
    whole = pl.BlockSpec(memory_space=pltpu.VMEM)
    return pl.pallas_call(
        functools.partial(gram_kernel, start),
        in_specs=[whole] * (len(pieces) + 4),
        out_specs=[whole] * 3,
        out_shape=[
            jax.ShapeDtypeStruct(before.shape, F32),
            jax.ShapeDtypeStruct((count, TIME, points), BF16),
            jax.ShapeDtypeStruct((count, points), F32),
        ],
        scratch_shapes=[
            pltpu.VMEM((GROUPS, ROWS * GROUP, count * WIDE), BF16),
            pltpu.VMEM((GROUPS, ROWS * GROUP, ROWS * GROUP), F32),
        ],
        compiler_params=pltpu.CompilerParams(vmem_limit_bytes=GRAM_VMEM),
        cost_estimate=pl.CostEstimate(
            flops=4 * points * count * (2 * NFFT * NFFT * BLOCKS + ROWS * ROWS * GROUP * FREQS),
            bytes_accessed=4 * count * TIME * points,
            transcendentals=0,
        ),
    )(*pieces, weights.reshape(1, -1), split, sums, before)


def turn(a, by):
    by = by % ROWS
    return a if by == 0 else jnp.concatenate([a[by:], a[:by]], axis=0)


def lanes(a, by):
    by = by % FREQS
    return a if by == 0 else pltpu.roll(a, by, 1)


def full_gram(packed):
    part = lax.broadcasted_iota(jnp.int32, (ROWS, FREQS), 1) // GROUP
    row = lax.broadcasted_iota(jnp.int32, (ROWS, FREQS), 0)
    out = []
    for k in range(BLOCKS):
        total = jnp.zeros((ROWS, FREQS), F32)
        for g in range(GROUPS):
            moved = lanes(packed[g * ROWS : (g + 1) * ROWS], (g - k) * GROUP)
            total = jnp.where(part == g, moved, total)
        out.append(total)
    rest = packed[GROUPS * ROWS :]
    total = jnp.zeros((ROWS, FREQS), F32)
    for delta in range(1 - BLOCKS, BLOCKS):
        moved = lanes(turn(rest, delta), delta * GROUP)
        total = jnp.where((row < BLOCKS) & (part - row == delta), moved, total)
    out.append(total + turn(total, BLOCKS))
    for k in range(BLOCKS + 1, ROWS):
        out.append(turn(out[ROWS - k], k))
    return out


def power_step(spectra, vector):
    return sum(spectra[k] * turn(vector, k) for k in range(ROWS))


def modes_kernel(packed_ref, table_ref, *refs):
    x_refs, mean_refs = refs[:2], refs[2:4]
    modes_ref, spectra_ref, m_ref, sum_ref, out_ref, sem_ref = refs[4:]
    count, _, half = x_refs[0].shape
    gram = full_gram(packed_ref[...])
    trace = jnp.sum(gram[0], axis=0, keepdims=True) + 1e-06
    spectra = [k * (2.0 * BLOCKS / trace) for k in gram]
    row = lax.broadcasted_iota(jnp.int32, (ROWS, FREQS), 0)
    for d in range(ROWS):
        total = jnp.zeros((ROWS, FREQS), F32)
        for c in range(ROWS):
            total = jnp.where(row == c, spectra[(d - c) % ROWS], total)
        spectra_ref[d * ROWS : (d + 1) * ROWS, :] = total
    first = power_step(spectra, jnp.ones((ROWS, FREQS), F32))
    lead = power_step(spectra, first) * (1.0 / math.sqrt(2.0 * BLOCKS))
    padded = jnp.concatenate([lead, jnp.zeros((FREQS - ROWS, FREQS), F32)], axis=0)
    lead = padded.T
    total = [jnp.zeros((FREQS, HOP), F32) for _ in range(BLOCKS + 1)]
    for b in range(BLOCKS):
        for r in range(2):
            c = r * BLOCKS + b
            part = lead[:, c : c + 1] * table_ref[r * FREQS : (r + 1) * FREQS, :]
            total[b] = total[b] + part[:, :HOP]
            total[b + 1] = total[b + 1] + part[:, HOP:]
    total = jnp.concatenate(total, axis=1)
    high = total.astype(BF16)
    low = (total - high.astype(F32)).astype(BF16)
    m_ref[:FREQS] = high
    m_ref[FREQS:] = low
    sum_ref[...] = jnp.sum(high.astype(F32) + low.astype(F32), axis=1, keepdims=True)

    copies = []
    for tile in range(2 * half // WIDE):
        part, at = divmod(tile * WIDE, half)
        out = []
        for v in range(count):
            x = x_refs[part][v, :, at : at + WIDE]
            both = jnp.dot(m_ref[...], x, preferred_element_type=F32)
            shift = sum_ref[...] * mean_refs[part][v : v + 1, at : at + WIDE]
            out.append((both[:FREQS] + both[FREQS:] - shift).astype(BF16))
        out_ref[tile] = pltpu.einshape("vfp->fvp", jnp.stack(out, 0))
        copy = pltpu.make_async_copy(
            out_ref.at[tile], modes_ref.at[:, :, pl.ds(tile * WIDE, WIDE)], sem_ref.at[tile]
        )
        copy.start()
        copies.append(copy)
    for copy in copies:
        copy.wait()


def modes_of(packed, table, series, means):
    count, _, half = series[0].shape
    whole = pl.BlockSpec(memory_space=pltpu.VMEM)
    tiles = 2 * half // WIDE
    return pl.pallas_call(
        modes_kernel,
        in_specs=[whole] * 6,
        out_specs=[pl.BlockSpec(memory_space=pl.ANY), whole],
        out_shape=[
            jax.ShapeDtypeStruct((FREQS, count, 2 * half), BF16),
            jax.ShapeDtypeStruct((ROWS * ROWS, FREQS), F32),
        ],
        scratch_shapes=[
            pltpu.VMEM((2 * FREQS, TIME), BF16),
            pltpu.VMEM((FREQS, 1), F32),
            pltpu.VMEM((tiles, FREQS, count, WIDE), BF16),
            pltpu.SemaphoreType.DMA((tiles,)),
        ],
        compiler_params=pltpu.CompilerParams(vmem_limit_bytes=GRAM_VMEM),
    )(packed, table, *series, *means)


def place(space, tm):
    z, low, core = space // 4, space // 2 % 2, space % 2
    return z, tm // ACROSS * 2 + low, tm % ACROSS, core


def device_at(z, y, x, core):
    return (z * 4 + y % 2 * 2 + core) * 8 + y // 2 * ACROSS + x


def sum_over_devices(value):
    rounds = [[(0, 0, 0, 1)]]
    rounds += [[tuple(k * (a == axis) for a in range(4)) for k in (1, 2, 3)] for axis in (2, 1, 0)]
    for flips in rounds:
        total = value
        for flip in flips:
            pairs = []
            for i in range(128):
                here = place(i // 8, i % 8)
                pairs.append((i, device_at(*(a ^ b for a, b in zip(here, flip)))))
            total = total + lax.ppermute(value, AXES, pairs)
        value = total
    return value


def per_device(members, devices, snapshots, weights):
    table, split, sums = tables()
    split, sums = jnp.asarray(split), jnp.asarray(sums)
    pieces = []
    for first, end in zip((0,) + PACKS[:-1], PACKS):
        pieces += pack(snapshots, first, end)
    sent = []
    for part in range(2):
        for k, step in enumerate(STEPS[:-1]):
            if part < parts_of(k):
                piece = pieces[k][part]
                if len(sent) >= DEPTH:
                    piece = lax.optimization_barrier((piece, sent[-DEPTH]))[0]
                pairs = [(m, shifted(m, step)) for m in range(members)]
                pieces[k][part] = lax.ppermute(piece, "tm", pairs)
                sent.append(pieces[k][part])
    half = weights.shape[0] // 2
    gram = jnp.zeros(((GROUPS + 1) * ROWS, FREQS), F32)
    series, means = [], []
    for part in range(2):
        mine = [piece[part % len(piece)] for piece in pieces]
        gram, x, mean = gram_terms(mine, weights, split, sums, gram, part * half, half)
        series.append(x)
        means.append(mean)
    gram = sum_over_devices(gram)
    modes, spectra = modes_of(gram, jnp.asarray(table), series, means)
    spectra = spectra.T.reshape(FREQS, ROWS, ROWS)
    return (modes, spectra)


def solution(mesh):
    members = mesh.shape["tm"]
    devices = members * mesh.shape["space"]
    in_specs = (P("tm", None, "space"), P(AXES))
    out_specs = (P(None, None, AXES), P())
    return jax.shard_map(
        functools.partial(per_device, members, devices),
        mesh=mesh,
        in_specs=in_specs,
        out_specs=out_specs,
        check_vma=False,
    )
```

profile of v0, /device:TPU:0, one launch (start us, length us, event | category | flops | bytes accessed | tf_op | source)
XLA Modules:
  0.0 105.4 jit_solution(14604159761799843189)
XLA Ops:
  0.6 2.4 %shard_map.68 = (bf16[4,80,1024]{2,1,0:T(8,128)(2,1)}, bf16[4,80,1024]{2,1,0:T(8,128)(2,1)}) custom-call(bf16[80,4,8192]{2,1,0:T(4,128)(2,1)} %x_ref.5), custom_call_target="tpu_custom_call" | custom-call | tf_op jit(solution)/shard_map/pallas_call | solution.py:83
  3.0 4.3 %collective-permute-start = (bf16[4,80,1024]{2,1,0:T(8,128)(2,1)}, bf16[4,80,1024]{2,1,0:T(8,128)(2,1)S(1)}, u32[]{:S(2)}, u32[]{:S(2)}) collective-permute-start(bf16[4,80,1024]{2,1,0:T(8,128)(2,1)} %get-tuple-element.19), channel_id=1, source_target_pairs={{0,5},{1,6},{2,7},{3,4},{4,1},{5,2},{6,3},{7,0},{8,13},{9,14},{10,... | collective-permute-start | bytes 1966088 | tf_op jit(solution)/shard_map/ppermute | solution.py:335
  7.3 0.0 copy-start
  7.3 1.7 %collective-permute-start.1 = (bf16[4,80,1024]{2,1,0:T(8,128)(2,1)}, bf16[4,80,1024]{2,1,0:T(8,128)(2,1)S(1)}, u32[]{:S(2)}, u32[]{:S(2)}) collective-permute-start(bf16[4,80,1024]{2,1,0:T(8,128)(2,1)} %get-tuple-element.20), channel_id=1, source_target_pairs={{0,3},{1,0},{2,1},{3,2},{4,7},{5,4},{6,5},{7,6},{8,11},{9,8},{10,9... | collective-permute-start | bytes 1966088 | tf_op jit(solution)/shard_map/ppermute | solution.py:335
  9.0 3.6 %shard_map.69 = (bf16[4,80,1024]{2,1,0:T(8,128)(2,1)}, bf16[4,80,1024]{2,1,0:T(8,128)(2,1)}, bf16[4,80,1024]{2,1,0:T(8,128)(2,1)}, bf16[4,80,1024]{2,1,0:T(8,128)(2,1)}, bf16[4,80,1024]{2,1,0:T(8,128)(2,1)}) custom-call(bf16[80,4,8192]{2,1,0:T(4,128)(2,1)} %x_ref.5), custom_call_target="tpu_custom_call" | custom-call | tf_op jit(solution)/shard_map/pallas_call | solution.py:83
  12.7 0.3 collective-permute-start.2
  13.0 2.3 %collective-permute-start.3 = (bf16[4,80,1024]{2,1,0:T(8,128)(2,1)}, bf16[4,80,1024]{2,1,0:T(8,128)(2,1)S(1)}, u32[]{:S(2)}, u32[]{:S(2)}) collective-permute-start(bf16[4,80,1024]{2,1,0:T(8,128)(2,1)} %get-tuple-element.22), channel_id=1, source_target_pairs={{0,2},{1,3},{2,0},{3,1},{4,6},{5,7},{6,4},{7,5},{8,10},{9,11},{10,... | collective-permute-start | bytes 1966088 | tf_op jit(solution)/shard_map/ppermute | solution.py:335
  15.3 4.0 %collective-permute-start.4 = (bf16[4,80,1024]{2,1,0:T(8,128)(2,1)}, bf16[4,80,1024]{2,1,0:T(8,128)(2,1)S(1)}, u32[]{:S(2)}, u32[]{:S(2)}) collective-permute-start(bf16[4,80,1024]{2,1,0:T(8,128)(2,1)} %get-tuple-element.23), channel_id=1, source_target_pairs={{0,6},{1,7},{2,4},{3,5},{4,2},{5,3},{6,0},{7,1},{8,14},{9,15},{10,... | collective-permute-start | bytes 1966088 | tf_op jit(solution)/shard_map/ppermute | solution.py:335
  19.2 4.5 %collective-permute-done.refs_0_ = bf16[4,80,1024]{2,1,0:T(8,128)(2,1)S(1)} collective-permute-done((bf16[4,80,1024]{2,1,0:T(8,128)(2,1)}, bf16[4,80,1024]{2,1,0:T(8,128)(2,1)S(1)}, u32[]{:S(2)}, u32[]{:S(2)}) %collective-permute-start) | collective-permute-done | bytes 655392 | tf_op jit(solution)/shard_map/ppermute | solution.py:335
  23.7 26.0 %collective-permute-done.1.refs_1_ = bf16[4,80,1024]{2,1,0:T(8,128)(2,1)S(1)} collective-permute-done((bf16[4,80,1024]{2,1,0:T(8,128)(2,1)}, bf16[4,80,1024]{2,1,0:T(8,128)(2,1)S(1)}, u32[]{:S(2)}, u32[]{:S(2)}) %collective-permute-start.1) | collective-permute-done | bytes 655392 | tf_op jit(solution)/shard_map/ppermute | solution.py:335
  49.8 0.0 copy-start.2
  49.8 0.0 copy-start.3
  49.8 0.0 copy-start.4
  49.8 4.2 %collective-permute-start.6 = (bf16[4,80,1024]{2,1,0:T(8,128)(2,1)}, bf16[4,80,1024]{2,1,0:T(8,128)(2,1)S(1)}, u32[]{:S(2)}, u32[]{:S(2)}) collective-permute-start(bf16[4,80,1024]{2,1,0:T(8,128)(2,1)} %get-tuple-element.27), channel_id=1, source_target_pairs={{0,7},{1,4},{2,5},{3,6},{4,3},{5,0},{6,1},{7,2},{8,15},{9,12},{10,... | collective-permute-start | bytes 1966088 | tf_op jit(solution)/shard_map/ppermute | solution.py:335
  54.0 0.0 collective-permute-start.5
  54.0 0.0 copy-done
  54.0 0.3 shard_map.70.refs_7_
  54.3 0.0 collective-permute-done.2.refs_2_
  54.3 0.0 collective-permute-done.3.refs_3_
  54.4 0.3 collective-permute-done.4.refs_4_
  54.6 12.1 %collective-permute-done.6.refs_6_ = bf16[4,80,1024]{2,1,0:T(8,128)(2,1)S(1)} collective-permute-done((bf16[4,80,1024]{2,1,0:T(8,128)(2,1)}, bf16[4,80,1024]{2,1,0:T(8,128)(2,1)S(1)}, u32[]{:S(2)}, u32[]{:S(2)}) %collective-permute-start.6) | collective-permute-done | bytes 655392 | tf_op jit(solution)/shard_map/ppermute | solution.py:335
  66.7 0.1 collective-permute-done.5.refs_5_
  66.9 0.0 copy-done.2
  66.9 0.0 copy-done.3
  66.9 0.0 copy-done.4
  66.9 4.2 %shard_map.71 = (f32[40,128]{1,0:T(8,128)S(1)}, bf16[4,640,512]{2,1,0:T(8,128)(2,1)S(1)}, f32[4,512]{1,0:T(4,128)S(1)}) custom-call(bf16[4,80,1024]{2,1,0:T(8,128)(2,1)S(1)} %collective-permute-done.refs_0_, bf16[4,80,1024]{2,1,0:T(8,128)(2,1)S(1)} %collective-permute-done.1.refs_1_, bf16[4,80,1024]{2,1,0:T(8,128)(2,1)S(1)} %collective-permute-done.2.refs_2_, ...), custom_call_target="tpu_custom_call" | custom-call | flops 6442450944 | bytes 5242880 | tf_op jit(solution)/shard_map/pallas_call | solution.py:168
  71.1 0.0 copy-start.1
  71.1 4.1 %shard_map.72 = (f32[40,128]{1,0:T(8,128)S(1)}, bf16[4,640,512]{2,1,0:T(8,128)(2,1)S(1)}, f32[4,512]{1,0:T(4,128)S(1)}) custom-call(bf16[4,80,1024]{2,1,0:T(8,128)(2,1)S(1)} %collective-permute-done.refs_0_, bf16[4,80,1024]{2,1,0:T(8,128)(2,1)S(1)} %collective-permute-done.1.refs_1_, bf16[4,80,1024]{2,1,0:T(8,128)(2,1)S(1)} %collective-permute-done.2.refs_2_, ...), custom_call_target="tpu_custom_call" | custom-call | flops 6442450944 | bytes 5242880 | tf_op jit(solution)/shard_map/pallas_call | solution.py:168
  75.2 0.3 collective-permute-start.7
  75.5 1.2 %collective-permute-done.7 = f32[40,128]{1,0:T(8,128)S(1)} collective-permute-done((f32[40,128]{1,0:T(8,128)S(1)}, f32[40,128]{1,0:T(8,128)S(1)}, u32[]{:S(2)}, u32[]{:S(2)}) %collective-permute-start.7) | collective-permute-done | bytes 20512 | tf_op jit(solution)/shard_map/ppermute | solution.py:316
  76.7 1.8 %collective-permute-start.10 = (f32[40,128]{1,0:T(8,128)S(1)}, f32[40,128]{1,0:T(8,128)S(1)}, u32[]{:S(2)}, u32[]{:S(2)}) collective-permute-start(f32[40,128]{1,0:T(8,128)S(1)} %add.30), channel_id=1, source_target_pairs={{0,3},{1,2},{2,1},{3,0},{4,7},{5,6},{6,5},{7,4},{8,11},{9,10},{10,... | collective-permute-start | bytes 61448 | tf_op jit(solution)/shard_map/ppermute | solution.py:316
  78.5 1.1 %collective-permute-start.9 = (f32[40,128]{1,0:T(8,128)S(1)}, f32[40,128]{1,0:T(8,128)S(1)}, u32[]{:S(2)}, u32[]{:S(2)}) collective-permute-start(f32[40,128]{1,0:T(8,128)S(1)} %add.30), channel_id=1, source_target_pairs={{0,2},{1,3},{2,0},{3,1},{4,6},{5,7},{6,4},{7,5},{8,10},{9,11},{10,... | collective-permute-start | bytes 61448 | tf_op jit(solution)/shard_map/ppermute | solution.py:316
  79.6 1.2 %collective-permute-start.8 = (f32[40,128]{1,0:T(8,128)S(1)}, f32[40,128]{1,0:T(8,128)S(1)}, u32[]{:S(2)}, u32[]{:S(2)}) collective-permute-start(f32[40,128]{1,0:T(8,128)S(1)} %add.30), channel_id=1, source_target_pairs={{0,1},{1,0},{2,3},{3,2},{4,5},{5,4},{6,7},{7,6},{8,9},{9,8},{10,11... | collective-permute-start | bytes 61448 | tf_op jit(solution)/shard_map/ppermute | solution.py:316
  80.8 0.9 collective-permute-done.10
  81.7 2.1 %collective-permute-done.9 = f32[40,128]{1,0:T(8,128)S(1)} collective-permute-done((f32[40,128]{1,0:T(8,128)S(1)}, f32[40,128]{1,0:T(8,128)S(1)}, u32[]{:S(2)}, u32[]{:S(2)}) %collective-permute-start.9) | collective-permute-done | bytes 20512 | tf_op jit(solution)/shard_map/ppermute | solution.py:316
  83.8 0.0 collective-permute-done.8
  83.8 3.0 %collective-permute-start.13 = (f32[40,128]{1,0:T(8,128)S(1)}, f32[40,128]{1,0:T(8,128)S(1)}, u32[]{:S(2)}, u32[]{:S(2)}) collective-permute-start(f32[40,128]{1,0:T(8,128)S(1)} %add_add_fusion.2), channel_id=1, source_target_pairs={{0,20},{1,21},{2,22},{3,23},{4,16},{5,17},{6,18},{7,19},{8,28},{9,... | collective-permute-start | bytes 61448 | tf_op jit(solution)/shard_map/ppermute | solution.py:316
  86.8 0.6 collective-permute-start.12
  87.4 0.6 collective-permute-start.11
  88.0 0.9 collective-permute-done.13
  88.9 3.2 %collective-permute-done.12 = f32[40,128]{1,0:T(8,128)S(1)} collective-permute-done((f32[40,128]{1,0:T(8,128)S(1)}, f32[40,128]{1,0:T(8,128)S(1)}, u32[]{:S(2)}, u32[]{:S(2)}) %collective-permute-start.12) | collective-permute-done | bytes 20512 | tf_op jit(solution)/shard_map/ppermute | solution.py:316
  92.1 0.0 collective-permute-done.11
  92.1 4.1 %collective-permute-start.16 = (f32[40,128]{1,0:T(8,128)S(1)}, f32[40,128]{1,0:T(8,128)S(1)}, u32[]{:S(2)}, u32[]{:S(2)}) collective-permute-start(f32[40,128]{1,0:T(8,128)S(1)} %add_add_fusion.1), channel_id=1, source_target_pairs={{0,96},{1,97},{2,98},{3,99},{4,100},{5,101},{6,102},{7,103},{8,104... | collective-permute-start | bytes 61448 | tf_op jit(solution)/shard_map/ppermute | solution.py:316
  96.2 0.0 collective-permute-start.15
  96.2 0.9 collective-permute-start.14
  97.2 0.8 collective-permute-done.16
  98.0 3.5 %collective-permute-done.15 = f32[40,128]{1,0:T(8,128)S(1)} collective-permute-done((f32[40,128]{1,0:T(8,128)S(1)}, f32[40,128]{1,0:T(8,128)S(1)}, u32[]{:S(2)}, u32[]{:S(2)}) %collective-permute-start.15) | collective-permute-done | bytes 20512 | tf_op jit(solution)/shard_map/ppermute | solution.py:316
  101.5 0.0 collective-permute-done.14
  101.5 0.0 copy-done.1
  101.5 3.7 %shard_map.73 = (bf16[128,4,1024]{2,1,0:T(4,128)(2,1)}, f32[64,128]{1,0:T(8,128)}) custom-call(f32[40,128]{1,0:T(8,128)S(1)} %add_add_fusion.packed_ref, f32[256,256]{1,0:T(8,128)S(1)} %copy-done.1, bf16[4,640,512]{2,1,0:T(8,128)(2,1)S(1)} %get-tuple-element.30.refs_0_, bf16[4,640,512]{2,1,0:T(8,128)(2,1)S(1)} %get-tuple-element.31.refs_1_, ...), custom_call_target="tpu_custom_call" | custom-call | tf_op jit(solution)/shard_map/pallas_call | solution.py:279
  (5 shorter events, 0.0 us)
Async XLA Ops:
  3.0 20.7 %collective-permute-start = (bf16[4,80,1024]{2,1,0:T(8,128)(2,1)}, bf16[4,80,1024]{2,1,0:T(8,128)(2,1)S(1)}, u32[]{:S(2)}, u32[]{:S(2)}) collective-permute-start(bf16[4,80,1024]{2,1,0:T(8,128)(2,1)} %get-tuple-element.19), channel_id=1, source_target_pairs={{0,5},{1,6},{2,7},{3,4},{4,1},{5,2},{6,3},{7,0},{8,13},{9,14},{10,... | collective-permute-start | bytes 1966088 | tf_op jit(solution)/shard_map/ppermute | solution.py:335
  7.3 46.7 %copy-start = (bf16[80,4,8192]{2,1,0:T(4,128)(2,1)S(1)}, bf16[80,4,8192]{2,1,0:T(4,128)(2,1)}, u32[]{:S(2)}) copy-start(bf16[80,4,8192]{2,1,0:T(4,128)(2,1)} %x_ref.5) | copy-start | bytes 15728644
  7.3 42.5 %collective-permute-start.1 = (bf16[4,80,1024]{2,1,0:T(8,128)(2,1)}, bf16[4,80,1024]{2,1,0:T(8,128)(2,1)S(1)}, u32[]{:S(2)}, u32[]{:S(2)}) collective-permute-start(bf16[4,80,1024]{2,1,0:T(8,128)(2,1)} %get-tuple-element.20), channel_id=1, source_target_pairs={{0,3},{1,0},{2,1},{3,2},{4,7},{5,4},{6,5},{7,6},{8,11},{9,8},{10,9... | collective-permute-start | bytes 1966088 | tf_op jit(solution)/shard_map/ppermute | solution.py:335
  12.7 41.7 %collective-permute-start.2 = (bf16[4,80,1024]{2,1,0:T(8,128)(2,1)}, bf16[4,80,1024]{2,1,0:T(8,128)(2,1)S(1)}, u32[]{:S(2)}, u32[]{:S(2)}) collective-permute-start(bf16[4,80,1024]{2,1,0:T(8,128)(2,1)} %get-tuple-element.21), channel_id=1, source_target_pairs={{0,4},{1,5},{2,6},{3,7},{4,0},{5,1},{6,2},{7,3},{8,12},{9,13},{10,... | collective-permute-start | bytes 1966088 | tf_op jit(solution)/shard_map/ppermute | solution.py:335
  13.0 41.3 %collective-permute-start.3 = (bf16[4,80,1024]{2,1,0:T(8,128)(2,1)}, bf16[4,80,1024]{2,1,0:T(8,128)(2,1)S(1)}, u32[]{:S(2)}, u32[]{:S(2)}) collective-permute-start(bf16[4,80,1024]{2,1,0:T(8,128)(2,1)} %get-tuple-element.22), channel_id=1, source_target_pairs={{0,2},{1,3},{2,0},{3,1},{4,6},{5,7},{6,4},{7,5},{8,10},{9,11},{10,... | collective-permute-start | bytes 1966088 | tf_op jit(solution)/shard_map/ppermute | solution.py:335
  15.3 39.4 %collective-permute-start.4 = (bf16[4,80,1024]{2,1,0:T(8,128)(2,1)}, bf16[4,80,1024]{2,1,0:T(8,128)(2,1)S(1)}, u32[]{:S(2)}, u32[]{:S(2)}) collective-permute-start(bf16[4,80,1024]{2,1,0:T(8,128)(2,1)} %get-tuple-element.23), channel_id=1, source_target_pairs={{0,6},{1,7},{2,4},{3,5},{4,2},{5,3},{6,0},{7,1},{8,14},{9,15},{10,... | collective-permute-start | bytes 1966088 | tf_op jit(solution)/shard_map/ppermute | solution.py:335
  49.8 17.1 %copy-start.2 = (f32[1024]{0:T(1024)S(1)}, f32[1024]{0:T(1024)}, u32[]{:S(2)}) copy-start(f32[1024]{0:T(1024)} %param.6) | copy-start | bytes 12292
  49.8 17.1 %copy-start.3 = (bf16[512,256]{1,0:T(8,128)(2,1)S(1)}, bf16[512,256]{1,0:T(8,128)(2,1)}, u32[]{:S(2)}) copy-start(bf16[512,256]{1,0:T(8,128)(2,1)} %constant.8.clone.refs_9_) | copy-start | bytes 786436
  49.8 17.1 %copy-start.4 = (f32[256,1]{1,0:T(8,128)S(1)}, f32[256,1]{1,0:T(8,128)}, u32[]{:S(2)}) copy-start(f32[256,1]{1,0:T(8,128)} %constant.9.clone.refs_10_) | copy-start | bytes 3076
  49.8 16.9 %collective-permute-start.6 = (bf16[4,80,1024]{2,1,0:T(8,128)(2,1)}, bf16[4,80,1024]{2,1,0:T(8,128)(2,1)S(1)}, u32[]{:S(2)}, u32[]{:S(2)}) collective-permute-start(bf16[4,80,1024]{2,1,0:T(8,128)(2,1)} %get-tuple-element.27), channel_id=1, source_target_pairs={{0,7},{1,4},{2,5},{3,6},{4,3},{5,0},{6,1},{7,2},{8,15},{9,12},{10,... | collective-permute-start | bytes 1966088 | tf_op jit(solution)/shard_map/ppermute | solution.py:335
  54.0 12.9 %collective-permute-start.5 = (bf16[4,80,1024]{2,1,0:T(8,128)(2,1)}, bf16[4,80,1024]{2,1,0:T(8,128)(2,1)S(1)}, u32[]{:S(2)}, u32[]{:S(2)}) collective-permute-start(bf16[4,80,1024]{2,1,0:T(8,128)(2,1)} %get-tuple-element.25), channel_id=1, source_target_pairs={{0,1},{1,2},{2,3},{3,0},{4,5},{5,6},{6,7},{7,4},{8,9},{9,10},{10,1... | collective-permute-start | bytes 1966088 | tf_op jit(solution)/shard_map/ppermute | solution.py:335
  71.1 30.4 %copy-start.1 = (f32[256,256]{1,0:T(8,128)S(1)}, f32[256,256]{1,0:T(8,128)}, u32[]{:S(2)}) copy-start(f32[256,256]{1,0:T(8,128)} %constant.10.clone.table_ref) | copy-start | bytes 786436
  75.2 1.4 %collective-permute-start.7 = (f32[40,128]{1,0:T(8,128)S(1)}, f32[40,128]{1,0:T(8,128)S(1)}, u32[]{:S(2)}, u32[]{:S(2)}) collective-permute-start(f32[40,128]{1,0:T(8,128)S(1)} %get-tuple-element.29), channel_id=1, source_target_pairs={{0,8},{1,9},{2,10},{3,11},{4,12},{5,13},{6,14},{7,15},{8,0},{9,1},... | collective-permute-start | bytes 61448 | tf_op jit(solution)/shard_map/ppermute | solution.py:316
  76.7 5.0 %collective-permute-start.10 = (f32[40,128]{1,0:T(8,128)S(1)}, f32[40,128]{1,0:T(8,128)S(1)}, u32[]{:S(2)}, u32[]{:S(2)}) collective-permute-start(f32[40,128]{1,0:T(8,128)S(1)} %add.30), channel_id=1, source_target_pairs={{0,3},{1,2},{2,1},{3,0},{4,7},{5,6},{6,5},{7,4},{8,11},{9,10},{10,... | collective-permute-start | bytes 61448 | tf_op jit(solution)/shard_map/ppermute | solution.py:316
  78.5 5.3 %collective-permute-start.9 = (f32[40,128]{1,0:T(8,128)S(1)}, f32[40,128]{1,0:T(8,128)S(1)}, u32[]{:S(2)}, u32[]{:S(2)}) collective-permute-start(f32[40,128]{1,0:T(8,128)S(1)} %add.30), channel_id=1, source_target_pairs={{0,2},{1,3},{2,0},{3,1},{4,6},{5,7},{6,4},{7,5},{8,10},{9,11},{10,... | collective-permute-start | bytes 61448 | tf_op jit(solution)/shard_map/ppermute | solution.py:316
  79.6 4.2 %collective-permute-start.8 = (f32[40,128]{1,0:T(8,128)S(1)}, f32[40,128]{1,0:T(8,128)S(1)}, u32[]{:S(2)}, u32[]{:S(2)}) collective-permute-start(f32[40,128]{1,0:T(8,128)S(1)} %add.30), channel_id=1, source_target_pairs={{0,1},{1,0},{2,3},{3,2},{4,5},{5,4},{6,7},{7,6},{8,9},{9,8},{10,11... | collective-permute-start | bytes 61448 | tf_op jit(solution)/shard_map/ppermute | solution.py:316
  83.8 5.1 %collective-permute-start.13 = (f32[40,128]{1,0:T(8,128)S(1)}, f32[40,128]{1,0:T(8,128)S(1)}, u32[]{:S(2)}, u32[]{:S(2)}) collective-permute-start(f32[40,128]{1,0:T(8,128)S(1)} %add_add_fusion.2), channel_id=1, source_target_pairs={{0,20},{1,21},{2,22},{3,23},{4,16},{5,17},{6,18},{7,19},{8,28},{9,... | collective-permute-start | bytes 61448 | tf_op jit(solution)/shard_map/ppermute | solution.py:316
  86.8 5.3 %collective-permute-start.12 = (f32[40,128]{1,0:T(8,128)S(1)}, f32[40,128]{1,0:T(8,128)S(1)}, u32[]{:S(2)}, u32[]{:S(2)}) collective-permute-start(f32[40,128]{1,0:T(8,128)S(1)} %add_add_fusion.2), channel_id=1, source_target_pairs={{0,4},{1,5},{2,6},{3,7},{4,0},{5,1},{6,2},{7,3},{8,12},{9,13},{10,... | collective-permute-start | bytes 61448 | tf_op jit(solution)/shard_map/ppermute | solution.py:316
  87.4 4.7 %collective-permute-start.11 = (f32[40,128]{1,0:T(8,128)S(1)}, f32[40,128]{1,0:T(8,128)S(1)}, u32[]{:S(2)}, u32[]{:S(2)}) collective-permute-start(f32[40,128]{1,0:T(8,128)S(1)} %add_add_fusion.2), channel_id=1, source_target_pairs={{0,16},{1,17},{2,18},{3,19},{4,20},{5,21},{6,22},{7,23},{8,24},{9,... | collective-permute-start | bytes 61448 | tf_op jit(solution)/shard_map/ppermute | solution.py:316
  92.1 5.9 %collective-permute-start.16 = (f32[40,128]{1,0:T(8,128)S(1)}, f32[40,128]{1,0:T(8,128)S(1)}, u32[]{:S(2)}, u32[]{:S(2)}) collective-permute-start(f32[40,128]{1,0:T(8,128)S(1)} %add_add_fusion.1), channel_id=1, source_target_pairs={{0,96},{1,97},{2,98},{3,99},{4,100},{5,101},{6,102},{7,103},{8,104... | collective-permute-start | bytes 61448 | tf_op jit(solution)/shard_map/ppermute | solution.py:316
  96.2 5.3 %collective-permute-start.15 = (f32[40,128]{1,0:T(8,128)S(1)}, f32[40,128]{1,0:T(8,128)S(1)}, u32[]{:S(2)}, u32[]{:S(2)}) collective-permute-start(f32[40,128]{1,0:T(8,128)S(1)} %add_add_fusion.1), channel_id=1, source_target_pairs={{0,64},{1,65},{2,66},{3,67},{4,68},{5,69},{6,70},{7,71},{8,72},{9,... | collective-permute-start | bytes 61448 | tf_op jit(solution)/shard_map/ppermute | solution.py:316
  96.2 5.3 %collective-permute-start.14 = (f32[40,128]{1,0:T(8,128)S(1)}, f32[40,128]{1,0:T(8,128)S(1)}, u32[]{:S(2)}, u32[]{:S(2)}) collective-permute-start(f32[40,128]{1,0:T(8,128)S(1)} %add_add_fusion.1), channel_id=1, source_target_pairs={{0,32},{1,33},{2,34},{3,35},{4,36},{5,37},{6,38},{7,39},{8,40},{9,... | collective-permute-start | bytes 61448 | tf_op jit(solution)/shard_map/ppermute | solution.py:316
where the time goes:
time: 106 us; the launch traced here: 105 us
  waiting for transfers between devices  55.7 us (53%)
  starting transfers between devices  30.4 us (29%)
  Pallas kernels  18.4 us (17%)
    ppermute x7, waiting for transfers between devices, per_device(): pieces[k][part] = lax.ppermute(piece, 'tm', pairs)  43.1 us
    ppermute x7, starting transfers between devices, per_device(): pieces[k][part] = lax.ppermute(piece, 'tm', pairs)  16.8 us
    ppermute x10, starting transfers between devices, sum_over_devices(): total = total + lax.ppermute(value, AXES, pairs)  13.6 us
    ppermute x10, waiting for transfers between devices, sum_over_devices(): total = total + lax.ppermute(value, AXES, pairs)  12.6 us
    pallas_call x2, Pallas kernels, gram_terms(): pl.pallas_call(functools.partial(gram_kernel, start), in_specs=[whole] *...  8.34 us
    pallas_call x3, Pallas kernels, pack(): pl.pallas_call(functools.partial(pack_kernel, first, end), in_specs=[pl.B...  6.31 us
    pallas_call x1, Pallas kernels, modes_of(): pl.pallas_call(modes_kernel, in_specs=[whole] * 6, out_specs=[pl.BlockSpe...  3.72 us
  transfers between devices with their start and end apart: 17, of which 12 were waited for; matrix products, arithmetic and copies ran while one was open for 0% of the time, Pallas kernels for 4%

commit v1 on v0

--- a/solution.py
+++ b/solution.py
@@ -23,7 +23,7 @@
 WIDE = 512
 ACROSS = 4
 PACKS = (2, 7, 8)
-WHOLE = 7
+WHOLE = 5
 DEPTH = 5
 PACK_VMEM = 54 << 20
 GRAM_VMEM = 24 << 20

time: 106 us -> 102 us (0.962)
  waiting for transfers between devices: 55.7 us -> 46.3 us
  starting transfers between devices: 30.4 us -> 36 us
    ppermute x7 -> x9, waiting for transfers between devices: 43.1 us -> 33.7 us  [per_device(): pieces[k][part] = lax.ppermute(piece, 'tm', pairs)]
    ppermute x7 -> x9, starting transfers between devices: 16.8 us -> 22.6 us  [per_device(): pieces[k][part] = lax.ppermute(piece, 'tm', pairs)]
  transfers between devices with their start and end apart: 17 -> 19, of which waited for: 12 -> 11; matrix products, arithmetic and copies ran while one was open for 0% -> 0% of each run, Pallas kernels for 4% -> 8%
where the time goes in v1:
time: 102 us
  waiting for transfers between devices  46.3 us (45%)
  starting transfers between devices  36 us (35%)
  Pallas kernels  18.4 us (18%)
    ppermute x9, waiting for transfers between devices, per_device(): pieces[k][part] = lax.ppermute(piece, 'tm', pairs)  33.7 us
    ppermute x9, starting transfers between devices, per_device(): pieces[k][part] = lax.ppermute(piece, 'tm', pairs)  22.6 us
    ppermute x10, starting transfers between devices, sum_over_devices(): total = total + lax.ppermute(value, AXES, pairs)  13.4 us
    ppermute x10, waiting for transfers between devices, sum_over_devices(): total = total + lax.ppermute(value, AXES, pairs)  12.6 us
    pallas_call x2, Pallas kernels, gram_terms(): pl.pallas_call(functools.partial(gram_kernel, start), in_specs=[whole] *...  8.3 us
    pallas_call x3, Pallas kernels, pack(): pl.pallas_call(functools.partial(pack_kernel, first, end), in_specs=[pl.B...  6.33 us
    pallas_call x1, Pallas kernels, modes_of(): pl.pallas_call(modes_kernel, in_specs=[whole] * 6, out_specs=[pl.BlockSpe...  3.73 us
  transfers between devices with their start and end apart: 19, of which 11 were waited for; matrix products, arithmetic and copies ran while one was open for 0% of the time, Pallas kernels for 8%

profile of v1, /device:TPU:0, one launch (start us, length us, event | category | flops | bytes accessed | tf_op | source)
XLA Modules:
  0.0 101.7 jit_solution(10488059334863562464)
XLA Ops:
  0.6 2.4 %shard_map.68 = (bf16[4,80,1024]{2,1,0:T(8,128)(2,1)}, bf16[4,80,1024]{2,1,0:T(8,128)(2,1)}) custom-call(bf16[80,4,8192]{2,1,0:T(4,128)(2,1)} %x_ref.5), custom_call_target="tpu_custom_call" | custom-call | tf_op jit(solution)/shard_map/pallas_call | solution.py:83
  3.0 4.3 %collective-permute-start = (bf16[4,80,1024]{2,1,0:T(8,128)(2,1)}, bf16[4,80,1024]{2,1,0:T(8,128)(2,1)S(1)}, u32[]{:S(2)}, u32[]{:S(2)}) collective-permute-start(bf16[4,80,1024]{2,1,0:T(8,128)(2,1)} %get-tuple-element.23), channel_id=1, source_target_pairs={{0,5},{1,6},{2,7},{3,4},{4,1},{5,2},{6,3},{7,0},{8,13},{9,14},{10,... | collective-permute-start | bytes 1966088 | tf_op jit(solution)/shard_map/ppermute | solution.py:335
  7.3 0.0 copy-start
  7.3 1.7 %collective-permute-start.1 = (bf16[4,80,1024]{2,1,0:T(8,128)(2,1)}, bf16[4,80,1024]{2,1,0:T(8,128)(2,1)S(1)}, u32[]{:S(2)}, u32[]{:S(2)}) collective-permute-start(bf16[4,80,1024]{2,1,0:T(8,128)(2,1)} %get-tuple-element.24), channel_id=1, source_target_pairs={{0,3},{1,0},{2,1},{3,2},{4,7},{5,4},{6,5},{7,6},{8,11},{9,8},{10,9... | collective-permute-start | bytes 1966088 | tf_op jit(solution)/shard_map/ppermute | solution.py:335
  9.0 3.6 %shard_map.69 = (bf16[4,80,1024]{2,1,0:T(8,128)(2,1)}, bf16[4,80,1024]{2,1,0:T(8,128)(2,1)}, bf16[4,80,1024]{2,1,0:T(8,128)(2,1)}, bf16[4,80,512]{2,1,0:T(8,128)...) custom-call(bf16[80,4,8192]{2,1,0:T(4,128)(2,1)} %x_ref.5), custom_call_target="tpu_custom_call" | custom-call | tf_op jit(solution)/shard_map/pallas_call | solution.py:83
  12.7 0.3 collective-permute-start.2
  13.0 2.3 %collective-permute-start.3 = (bf16[4,80,1024]{2,1,0:T(8,128)(2,1)}, bf16[4,80,1024]{2,1,0:T(8,128)(2,1)S(1)}, u32[]{:S(2)}, u32[]{:S(2)}) collective-permute-start(bf16[4,80,1024]{2,1,0:T(8,128)(2,1)} %get-tuple-element.26), channel_id=1, source_target_pairs={{0,2},{1,3},{2,0},{3,1},{4,6},{5,7},{6,4},{7,5},{8,10},{9,11},{10,... | collective-permute-start | bytes 1966088 | tf_op jit(solution)/shard_map/ppermute | solution.py:335
  15.3 4.0 %collective-permute-start.4 = (bf16[4,80,1024]{2,1,0:T(8,128)(2,1)}, bf16[4,80,1024]{2,1,0:T(8,128)(2,1)S(1)}, u32[]{:S(2)}, u32[]{:S(2)}) collective-permute-start(bf16[4,80,1024]{2,1,0:T(8,128)(2,1)} %get-tuple-element.27), channel_id=1, source_target_pairs={{0,6},{1,7},{2,4},{3,5},{4,2},{5,3},{6,0},{7,1},{8,14},{9,15},{10,... | collective-permute-start | bytes 1966088 | tf_op jit(solution)/shard_map/ppermute | solution.py:335
  19.3 4.5 %collective-permute-done.refs_0_ = bf16[4,80,1024]{2,1,0:T(8,128)(2,1)S(1)} collective-permute-done((bf16[4,80,1024]{2,1,0:T(8,128)(2,1)}, bf16[4,80,1024]{2,1,0:T(8,128)(2,1)S(1)}, u32[]{:S(2)}, u32[]{:S(2)}) %collective-permute-start) | collective-permute-done | bytes 655392 | tf_op jit(solution)/shard_map/ppermute | solution.py:335
  23.7 26.0 %collective-permute-done.1.refs_1_ = bf16[4,80,1024]{2,1,0:T(8,128)(2,1)S(1)} collective-permute-done((bf16[4,80,1024]{2,1,0:T(8,128)(2,1)}, bf16[4,80,1024]{2,1,0:T(8,128)(2,1)S(1)}, u32[]{:S(2)}, u32[]{:S(2)}) %collective-permute-start.1) | collective-permute-done | bytes 655392 | tf_op jit(solution)/shard_map/ppermute | solution.py:335
  49.8 0.0 copy-start.6
  49.8 0.0 copy-start.5
  49.8 0.0 copy-start.2
  49.8 0.0 copy-start.3
  49.8 0.0 copy-start.4
  49.8 4.3 %collective-permute-start.8 = (bf16[4,80,512]{2,1,0:T(8,128)(2,1)}, bf16[4,80,512]{2,1,0:T(8,128)(2,1)S(1)}, u32[]{:S(2)}, u32[]{:S(2)}) collective-permute-start(bf16[4,80,512]{2,1,0:T(8,128)(2,1)} %get-tuple-element.35), channel_id=1, source_target_pairs={{0,7},{1,4},{2,5},{3,6},{4,3},{5,0},{6,1},{7,2},{8,15},{9,12},{10,... | collective-permute-start | bytes 983048 | tf_op jit(solution)/shard_map/ppermute | solution.py:335
  54.1 0.0 collective-permute-start.7
  54.1 0.0 copy-done
  54.1 0.3 shard_map.70.refs_7_
  54.4 0.0 collective-permute-done.2.refs_2_
  54.4 0.0 copy-done.6
  54.4 0.1 collective-permute-start.5
  54.5 0.0 collective-permute-done.3.refs_3_
  54.5 0.0 copy-done.5
  54.5 5.6 %collective-permute-start.6 = (bf16[4,80,512]{2,1,0:T(8,128)(2,1)S(1)}, bf16[4,80,512]{2,1,0:T(8,128)(2,1)S(1)}, u32[]{:S(2)}, u32[]{:S(2)}) collective-permute-start(bf16[4,80,512]{2,1,0:T(8,128)(2,1)S(1)} %copy-done.5), channel_id=1, source_target_pairs={{0,7},{1,4},{2,5},{3,6},{4,3},{5,0},{6,1},{7,2},{8,15},{9,12},{10,... | collective-permute-start | bytes 983048 | tf_op jit(solution)/shard_map/ppermute | solution.py:335
  60.2 0.0 collective-permute-done.4.refs_4_
  60.2 3.0 %collective-permute-done.8.refs_6_ = bf16[4,80,512]{2,1,0:T(8,128)(2,1)S(1)} collective-permute-done((bf16[4,80,512]{2,1,0:T(8,128)(2,1)}, bf16[4,80,512]{2,1,0:T(8,128)(2,1)S(1)}, u32[]{:S(2)}, u32[]{:S(2)}) %collective-permute-start.8) | collective-permute-done | bytes 327712 | tf_op jit(solution)/shard_map/ppermute | solution.py:335
  63.2 0.2 collective-permute-done.7.refs_5_
  63.3 0.0 copy-done.2
  63.3 0.0 copy-done.3
  63.4 0.0 copy-done.4
  63.4 4.2 %shard_map.71 = (f32[40,128]{1,0:T(8,128)S(1)}, bf16[4,640,512]{2,1,0:T(8,128)(2,1)S(1)}, f32[4,512]{1,0:T(4,128)S(1)}) custom-call(bf16[4,80,1024]{2,1,0:T(8,128)(2,1)S(1)} %collective-permute-done.refs_0_, bf16[4,80,1024]{2,1,0:T(8,128)(2,1)S(1)} %collective-permute-done.1.refs_1_, bf16[4,80,1024]{2,1,0:T(8,128)(2,1)S(1)} %collective-permute-done.2.refs_2_, ...), custom_call_target="tpu_custom_call" | custom-call | flops 6442450944 | bytes 5242880 | tf_op jit(solution)/shard_map/pallas_call | solution.py:168
  67.5 0.0 collective-permute-done.5.refs_5_
  67.5 0.0 collective-permute-done.6.refs_6_
  67.6 0.0 copy-start.1
  67.6 4.1 %shard_map.72 = (f32[40,128]{1,0:T(8,128)S(1)}, bf16[4,640,512]{2,1,0:T(8,128)(2,1)S(1)}, f32[4,512]{1,0:T(4,128)S(1)}) custom-call(bf16[4,80,1024]{2,1,0:T(8,128)(2,1)S(1)} %collective-permute-done.refs_0_, bf16[4,80,1024]{2,1,0:T(8,128)(2,1)S(1)} %collective-permute-done.1.refs_1_, bf16[4,80,1024]{2,1,0:T(8,128)(2,1)S(1)} %collective-permute-done.2.refs_2_, ...), custom_call_target="tpu_custom_call" | custom-call | flops 6442450944 | bytes 5242880 | tf_op jit(solution)/shard_map/pallas_call | solution.py:168
  71.7 0.1 collective-permute-start.9
  71.8 1.2 %collective-permute-done.9 = f32[40,128]{1,0:T(8,128)S(1)} collective-permute-done((f32[40,128]{1,0:T(8,128)S(1)}, f32[40,128]{1,0:T(8,128)S(1)}, u32[]{:S(2)}, u32[]{:S(2)}) %collective-permute-start.9) | collective-permute-done | bytes 20512 | tf_op jit(solution)/shard_map/ppermute | solution.py:316
  73.0 1.7 %collective-permute-start.12 = (f32[40,128]{1,0:T(8,128)S(1)}, f32[40,128]{1,0:T(8,128)S(1)}, u32[]{:S(2)}, u32[]{:S(2)}) collective-permute-start(f32[40,128]{1,0:T(8,128)S(1)} %add.30), channel_id=1, source_target_pairs={{0,3},{1,2},{2,1},{3,0},{4,7},{5,6},{6,5},{7,4},{8,11},{9,10},{10,... | collective-permute-start | bytes 61448 | tf_op jit(solution)/shard_map/ppermute | solution.py:316
  74.7 0.5 collective-permute-start.11
  75.2 1.9 %collective-permute-start.10 = (f32[40,128]{1,0:T(8,128)S(1)}, f32[40,128]{1,0:T(8,128)S(1)}, u32[]{:S(2)}, u32[]{:S(2)}) collective-permute-start(f32[40,128]{1,0:T(8,128)S(1)} %add.30), channel_id=1, source_target_pairs={{0,1},{1,0},{2,3},{3,2},{4,5},{5,4},{6,7},{7,6},{8,9},{9,8},{10,11... | collective-permute-start | bytes 61448 | tf_op jit(solution)/shard_map/ppermute | solution.py:316
  77.1 0.9 collective-permute-done.12
  78.0 2.0 %collective-permute-done.11 = f32[40,128]{1,0:T(8,128)S(1)} collective-permute-done((f32[40,128]{1,0:T(8,128)S(1)}, f32[40,128]{1,0:T(8,128)S(1)}, u32[]{:S(2)}, u32[]{:S(2)}) %collective-permute-start.11) | collective-permute-done | bytes 20512 | tf_op jit(solution)/shard_map/ppermute | solution.py:316
  80.0 0.0 collective-permute-done.10
  80.0 3.0 %collective-permute-start.15 = (f32[40,128]{1,0:T(8,128)S(1)}, f32[40,128]{1,0:T(8,128)S(1)}, u32[]{:S(2)}, u32[]{:S(2)}) collective-permute-start(f32[40,128]{1,0:T(8,128)S(1)} %add_add_fusion.2), channel_id=1, source_target_pairs={{0,20},{1,21},{2,22},{3,23},{4,16},{5,17},{6,18},{7,19},{8,28},{9,... | collective-permute-start | bytes 61448 | tf_op jit(solution)/shard_map/ppermute | solution.py:316
  83.0 0.6 collective-permute-start.14
  83.7 0.5 collective-permute-start.13
  84.2 0.9 collective-permute-done.15
  85.1 3.2 %collective-permute-done.14 = f32[40,128]{1,0:T(8,128)S(1)} collective-permute-done((f32[40,128]{1,0:T(8,128)S(1)}, f32[40,128]{1,0:T(8,128)S(1)}, u32[]{:S(2)}, u32[]{:S(2)}) %collective-permute-start.14) | collective-permute-done | bytes 20512 | tf_op jit(solution)/shard_map/ppermute | solution.py:316
  88.3 0.0 collective-permute-done.13
  88.3 4.1 %collective-permute-start.18 = (f32[40,128]{1,0:T(8,128)S(1)}, f32[40,128]{1,0:T(8,128)S(1)}, u32[]{:S(2)}, u32[]{:S(2)}) collective-permute-start(f32[40,128]{1,0:T(8,128)S(1)} %add_add_fusion.1), channel_id=1, source_target_pairs={{0,96},{1,97},{2,98},{3,99},{4,100},{5,101},{6,102},{7,103},{8,104... | collective-permute-start | bytes 61448 | tf_op jit(solution)/shard_map/ppermute | solution.py:316
  92.5 0.0 collective-permute-start.17
  92.5 0.9 collective-permute-start.16
  93.4 0.8 collective-permute-done.18
  94.2 3.5 %collective-permute-done.17 = f32[40,128]{1,0:T(8,128)S(1)} collective-permute-done((f32[40,128]{1,0:T(8,128)S(1)}, f32[40,128]{1,0:T(8,128)S(1)}, u32[]{:S(2)}, u32[]{:S(2)}) %collective-permute-start.17) | collective-permute-done | bytes 20512 | tf_op jit(solution)/shard_map/ppermute | solution.py:316
  97.7 0.0 collective-permute-done.16
  97.8 0.0 copy-done.1
  97.8 3.7 %shard_map.73 = (bf16[128,4,1024]{2,1,0:T(4,128)(2,1)}, f32[64,128]{1,0:T(8,128)}) custom-call(f32[40,128]{1,0:T(8,128)S(1)} %add_add_fusion.packed_ref, f32[256,256]{1,0:T(8,128)S(1)} %copy-done.1, bf16[4,640,512]{2,1,0:T(8,128)(2,1)S(1)} %get-tuple-element.38.refs_0_, bf16[4,640,512]{2,1,0:T(8,128)(2,1)S(1)} %get-tuple-element.39.refs_1_, ...), custom_call_target="tpu_custom_call" | custom-call | tf_op jit(solution)/shard_map/pallas_call | solution.py:279
  (5 shorter events, 0.0 us)
Async XLA Ops:
  3.0 20.7 %collective-permute-start = (bf16[4,80,1024]{2,1,0:T(8,128)(2,1)}, bf16[4,80,1024]{2,1,0:T(8,128)(2,1)S(1)}, u32[]{:S(2)}, u32[]{:S(2)}) collective-permute-start(bf16[4,80,1024]{2,1,0:T(8,128)(2,1)} %get-tuple-element.23), channel_id=1, source_target_pairs={{0,5},{1,6},{2,7},{3,4},{4,1},{5,2},{6,3},{7,0},{8,13},{9,14},{10,... | collective-permute-start | bytes 1966088 | tf_op jit(solution)/shard_map/ppermute | solution.py:335
  7.3 46.8 %copy-start = (bf16[80,4,8192]{2,1,0:T(4,128)(2,1)S(1)}, bf16[80,4,8192]{2,1,0:T(4,128)(2,1)}, u32[]{:S(2)}) copy-start(bf16[80,4,8192]{2,1,0:T(4,128)(2,1)} %x_ref.5) | copy-start | bytes 15728644
  7.3 42.5 %collective-permute-start.1 = (bf16[4,80,1024]{2,1,0:T(8,128)(2,1)}, bf16[4,80,1024]{2,1,0:T(8,128)(2,1)S(1)}, u32[]{:S(2)}, u32[]{:S(2)}) collective-permute-start(bf16[4,80,1024]{2,1,0:T(8,128)(2,1)} %get-tuple-element.24), channel_id=1, source_target_pairs={{0,3},{1,0},{2,1},{3,2},{4,7},{5,4},{6,5},{7,6},{8,11},{9,8},{10,9... | collective-permute-start | bytes 1966088 | tf_op jit(solution)/shard_map/ppermute | solution.py:335
  12.7 41.7 %collective-permute-start.2 = (bf16[4,80,1024]{2,1,0:T(8,128)(2,1)}, bf16[4,80,1024]{2,1,0:T(8,128)(2,1)S(1)}, u32[]{:S(2)}, u32[]{:S(2)}) collective-permute-start(bf16[4,80,1024]{2,1,0:T(8,128)(2,1)} %get-tuple-element.25), channel_id=1, source_target_pairs={{0,4},{1,5},{2,6},{3,7},{4,0},{5,1},{6,2},{7,3},{8,12},{9,13},{10,... | collective-permute-start | bytes 1966088 | tf_op jit(solution)/shard_map/ppermute | solution.py:335
  13.0 41.5 %collective-permute-start.3 = (bf16[4,80,1024]{2,1,0:T(8,128)(2,1)}, bf16[4,80,1024]{2,1,0:T(8,128)(2,1)S(1)}, u32[]{:S(2)}, u32[]{:S(2)}) collective-permute-start(bf16[4,80,1024]{2,1,0:T(8,128)(2,1)} %get-tuple-element.26), channel_id=1, source_target_pairs={{0,2},{1,3},{2,0},{3,1},{4,6},{5,7},{6,4},{7,5},{8,10},{9,11},{10,... | collective-permute-start | bytes 1966088 | tf_op jit(solution)/shard_map/ppermute | solution.py:335
  15.3 44.9 %collective-permute-start.4 = (bf16[4,80,1024]{2,1,0:T(8,128)(2,1)}, bf16[4,80,1024]{2,1,0:T(8,128)(2,1)S(1)}, u32[]{:S(2)}, u32[]{:S(2)}) collective-permute-start(bf16[4,80,1024]{2,1,0:T(8,128)(2,1)} %get-tuple-element.27), channel_id=1, source_target_pairs={{0,6},{1,7},{2,4},{3,5},{4,2},{5,3},{6,0},{7,1},{8,14},{9,15},{10,... | collective-permute-start | bytes 1966088 | tf_op jit(solution)/shard_map/ppermute | solution.py:335
  49.8 4.6 %copy-start.6 = (bf16[4,80,512]{2,1,0:T(8,128)(2,1)S(1)}, bf16[4,80,512]{2,1,0:T(8,128)(2,1)}, u32[]{:S(2)}) copy-start(bf16[4,80,512]{2,1,0:T(8,128)(2,1)} %get-tuple-element.29) | copy-start | bytes 983044
  49.8 4.7 %copy-start.5 = (bf16[4,80,512]{2,1,0:T(8,128)(2,1)S(1)}, bf16[4,80,512]{2,1,0:T(8,128)(2,1)}, u32[]{:S(2)}) copy-start(bf16[4,80,512]{2,1,0:T(8,128)(2,1)} %get-tuple-element.31) | copy-start | bytes 983044
  49.8 13.6 %copy-start.2 = (f32[1024]{0:T(1024)S(1)}, f32[1024]{0:T(1024)}, u32[]{:S(2)}) copy-start(f32[1024]{0:T(1024)} %param.6) | copy-start | bytes 12292
  49.8 13.6 %copy-start.3 = (bf16[512,256]{1,0:T(8,128)(2,1)S(1)}, bf16[512,256]{1,0:T(8,128)(2,1)}, u32[]{:S(2)}) copy-start(bf16[512,256]{1,0:T(8,128)(2,1)} %constant.8.clone.refs_9_) | copy-start | bytes 786436
  49.8 13.6 %copy-start.4 = (f32[256,1]{1,0:T(8,128)S(1)}, f32[256,1]{1,0:T(8,128)}, u32[]{:S(2)}) copy-start(f32[256,1]{1,0:T(8,128)} %constant.9.clone.refs_10_) | copy-start | bytes 3076
  49.8 13.4 %collective-permute-start.8 = (bf16[4,80,512]{2,1,0:T(8,128)(2,1)}, bf16[4,80,512]{2,1,0:T(8,128)(2,1)S(1)}, u32[]{:S(2)}, u32[]{:S(2)}) collective-permute-start(bf16[4,80,512]{2,1,0:T(8,128)(2,1)} %get-tuple-element.35), channel_id=1, source_target_pairs={{0,7},{1,4},{2,5},{3,6},{4,3},{5,0},{6,1},{7,2},{8,15},{9,12},{10,... | collective-permute-start | bytes 983048 | tf_op jit(solution)/shard_map/ppermute | solution.py:335
  54.1 9.3 %collective-permute-start.7 = (bf16[4,80,512]{2,1,0:T(8,128)(2,1)}, bf16[4,80,512]{2,1,0:T(8,128)(2,1)S(1)}, u32[]{:S(2)}, u32[]{:S(2)}) collective-permute-start(bf16[4,80,512]{2,1,0:T(8,128)(2,1)} %get-tuple-element.33), channel_id=1, source_target_pairs={{0,1},{1,2},{2,3},{3,0},{4,5},{5,6},{6,7},{7,4},{8,9},{9,10},{10,1... | collective-permute-start | bytes 983048 | tf_op jit(solution)/shard_map/ppermute | solution.py:335
  54.4 13.1 %collective-permute-start.5 = (bf16[4,80,512]{2,1,0:T(8,128)(2,1)S(1)}, bf16[4,80,512]{2,1,0:T(8,128)(2,1)S(1)}, u32[]{:S(2)}, u32[]{:S(2)}) collective-permute-start(bf16[4,80,512]{2,1,0:T(8,128)(2,1)S(1)} %copy-done.6), channel_id=1, source_target_pairs={{0,1},{1,2},{2,3},{3,0},{4,5},{5,6},{6,7},{7,4},{8,9},{9,10},{10,1... | collective-permute-start | bytes 983048 | tf_op jit(solution)/shard_map/ppermute | solution.py:335
  54.5 13.0 %collective-permute-start.6 = (bf16[4,80,512]{2,1,0:T(8,128)(2,1)S(1)}, bf16[4,80,512]{2,1,0:T(8,128)(2,1)S(1)}, u32[]{:S(2)}, u32[]{:S(2)}) collective-permute-start(bf16[4,80,512]{2,1,0:T(8,128)(2,1)S(1)} %copy-done.5), channel_id=1, source_target_pairs={{0,7},{1,4},{2,5},{3,6},{4,3},{5,0},{6,1},{7,2},{8,15},{9,12},{10,... | collective-permute-start | bytes 983048 | tf_op jit(solution)/shard_map/ppermute | solution.py:335
  67.6 30.2 %copy-start.1 = (f32[256,256]{1,0:T(8,128)S(1)}, f32[256,256]{1,0:T(8,128)}, u32[]{:S(2)}) copy-start(f32[256,256]{1,0:T(8,128)} %constant.10.clone.table_ref) | copy-start | bytes 786436
  71.7 1.3 %collective-permute-start.9 = (f32[40,128]{1,0:T(8,128)S(1)}, f32[40,128]{1,0:T(8,128)S(1)}, u32[]{:S(2)}, u32[]{:S(2)}) collective-permute-start(f32[40,128]{1,0:T(8,128)S(1)} %get-tuple-element.37), channel_id=1, source_target_pairs={{0,8},{1,9},{2,10},{3,11},{4,12},{5,13},{6,14},{7,15},{8,0},{9,1},... | collective-permute-start | bytes 61448 | tf_op jit(solution)/shard_map/ppermute | solution.py:316
  73.0 5.0 %collective-permute-start.12 = (f32[40,128]{1,0:T(8,128)S(1)}, f32[40,128]{1,0:T(8,128)S(1)}, u32[]{:S(2)}, u32[]{:S(2)}) collective-permute-start(f32[40,128]{1,0:T(8,128)S(1)} %add.30), channel_id=1, source_target_pairs={{0,3},{1,2},{2,1},{3,0},{4,7},{5,6},{6,5},{7,4},{8,11},{9,10},{10,... | collective-permute-start | bytes 61448 | tf_op jit(solution)/shard_map/ppermute | solution.py:316
  74.7 5.3 %collective-permute-start.11 = (f32[40,128]{1,0:T(8,128)S(1)}, f32[40,128]{1,0:T(8,128)S(1)}, u32[]{:S(2)}, u32[]{:S(2)}) collective-permute-start(f32[40,128]{1,0:T(8,128)S(1)} %add.30), channel_id=1, source_target_pairs={{0,2},{1,3},{2,0},{3,1},{4,6},{5,7},{6,4},{7,5},{8,10},{9,11},{10,... | collective-permute-start | bytes 61448 | tf_op jit(solution)/shard_map/ppermute | solution.py:316
  75.2 4.8 %collective-permute-start.10 = (f32[40,128]{1,0:T(8,128)S(1)}, f32[40,128]{1,0:T(8,128)S(1)}, u32[]{:S(2)}, u32[]{:S(2)}) collective-permute-start(f32[40,128]{1,0:T(8,128)S(1)} %add.30), channel_id=1, source_target_pairs={{0,1},{1,0},{2,3},{3,2},{4,5},{5,4},{6,7},{7,6},{8,9},{9,8},{10,11... | collective-permute-start | bytes 61448 | tf_op jit(solution)/shard_map/ppermute | solution.py:316
  80.0 5.1 %collective-permute-start.15 = (f32[40,128]{1,0:T(8,128)S(1)}, f32[40,128]{1,0:T(8,128)S(1)}, u32[]{:S(2)}, u32[]{:S(2)}) collective-permute-start(f32[40,128]{1,0:T(8,128)S(1)} %add_add_fusion.2), channel_id=1, source_target_pairs={{0,20},{1,21},{2,22},{3,23},{4,16},{5,17},{6,18},{7,19},{8,28},{9,... | collective-permute-start | bytes 61448 | tf_op jit(solution)/shard_map/ppermute | solution.py:316
  83.0 5.3 %collective-permute-start.14 = (f32[40,128]{1,0:T(8,128)S(1)}, f32[40,128]{1,0:T(8,128)S(1)}, u32[]{:S(2)}, u32[]{:S(2)}) collective-permute-start(f32[40,128]{1,0:T(8,128)S(1)} %add_add_fusion.2), channel_id=1, source_target_pairs={{0,4},{1,5},{2,6},{3,7},{4,0},{5,1},{6,2},{7,3},{8,12},{9,13},{10,... | collective-permute-start | bytes 61448 | tf_op jit(solution)/shard_map/ppermute | solution.py:316
  83.7 4.7 %collective-permute-start.13 = (f32[40,128]{1,0:T(8,128)S(1)}, f32[40,128]{1,0:T(8,128)S(1)}, u32[]{:S(2)}, u32[]{:S(2)}) collective-permute-start(f32[40,128]{1,0:T(8,128)S(1)} %add_add_fusion.2), channel_id=1, source_target_pairs={{0,16},{1,17},{2,18},{3,19},{4,20},{5,21},{6,22},{7,23},{8,24},{9,... | collective-permute-start | bytes 61448 | tf_op jit(solution)/shard_map/ppermute | solution.py:316
  88.3 5.9 %collective-permute-start.18 = (f32[40,128]{1,0:T(8,128)S(1)}, f32[40,128]{1,0:T(8,128)S(1)}, u32[]{:S(2)}, u32[]{:S(2)}) collective-permute-start(f32[40,128]{1,0:T(8,128)S(1)} %add_add_fusion.1), channel_id=1, source_target_pairs={{0,96},{1,97},{2,98},{3,99},{4,100},{5,101},{6,102},{7,103},{8,104... | collective-permute-start | bytes 61448 | tf_op jit(solution)/shard_map/ppermute | solution.py:316
  92.5 5.3 %collective-permute-start.17 = (f32[40,128]{1,0:T(8,128)S(1)}, f32[40,128]{1,0:T(8,128)S(1)}, u32[]{:S(2)}, u32[]{:S(2)}) collective-permute-start(f32[40,128]{1,0:T(8,128)S(1)} %add_add_fusion.1), channel_id=1, source_target_pairs={{0,64},{1,65},{2,66},{3,67},{4,68},{5,69},{6,70},{7,71},{8,72},{9,... | collective-permute-start | bytes 61448 | tf_op jit(solution)/shard_map/ppermute | solution.py:316
  92.5 5.3 %collective-permute-start.16 = (f32[40,128]{1,0:T(8,128)S(1)}, f32[40,128]{1,0:T(8,128)S(1)}, u32[]{:S(2)}, u32[]{:S(2)}) collective-permute-start(f32[40,128]{1,0:T(8,128)S(1)} %add_add_fusion.1), channel_id=1, source_target_pairs={{0,32},{1,33},{2,34},{3,35},{4,36},{5,37},{6,38},{7,39},{8,40},{9,... | collective-permute-start | bytes 61448 | tf_op jit(solution)/shard_map/ppermute | solution.py:316
